TPU v7x, 32 devices: a whole 2x2x4 slice. The times are simulated.
32 devices in a mesh: shoot: 4 (over y, x), gx: 8 (over z, core).
Axes of the slice: x: 2, y: 2, z: 4, core: 2. Of those that a mesh axis runs over, the one named last changes fastest.
Arguments:
- start_states: float32 [4, 256, 64, 128], P('shoot', 'gx'), may hold values from 0.35 to 0.85
- initial_state: float32 [256, 64, 128], P('gx'), may hold values from 0.35 to 0.85
- x_velocity: float32 [256, 64, 128], P('gx'), may hold values from -1 to 1
- y_velocity: float32 [256, 64, 128], P('gx'), may hold values from -0.2 to 0.2
- z_velocity: float32 [256, 64, 128], P('gx'), may hold values from -0.2 to 0.2
- step_scale: float32 [256, 64, 128], P('gx'), may hold values from 0.13 to 0.26
- well_cells: int32 [8, 16], P('gx'), may hold values from 65536 to 196607, as said below
- well_rates: float32 [8, 16], P('gx'), may hold values from -0.8 to 0.8
- roster: int32 [4, 8, 16], P('shoot', 'gx'), may hold values 0 or 1
Outputs:
- end_states: float32 [4, 256, 64, 128], P('shoot', 'gx')
- defects: float32 [4, 256, 64, 128], P('shoot', 'gx')
Inputs may be any that keep to these rules, and one draw needn't show every extreme that they name: `well_cells`: each entry is a flattened cell (x * 64 + z) * 128 + y of its own slab whose x lies from 8 to 23; cells may repeat.
All inputs are finite; a program needn't handle non-finite values. No bound on the sum of `roster` on one device may be relied on, other than what follows from the above.
Results may differ from a plain program's by a relative error of at most 0.00002.
Values sent between devices are 32-bit elements; how exact they have to be, the bound alone decides.
A program may use at most 128 MiB of HBM per device.

v0:
```python
import jax
import jax.numpy as jnp
from jax import lax
from jax.sharding import PartitionSpec as P

STEPS = 8


def passed_along(block, axis, distance):
    devices = range(lax.axis_size(axis))
    route = [(i - distance, i) for i in devices if i - distance in devices]
    return lax.ppermute(block, axis, route)


def extended_2(block, sides, width):
    for axis, dim in sides:
        count = lax.axis_size(axis)
        forward = [(i, i + 1) for i in range(count - 1)]
        backward = [(target, source) for source, target in forward]
        low = lax.ppermute(
            lax.slice_in_dim(block, block.shape[dim] - width, None, axis=dim), axis, forward
        )
        high = lax.ppermute(lax.slice_in_dim(block, 0, width, axis=dim), axis, backward)
        block = jnp.concatenate([low, block, high], axis=dim)
    return block


def fraction(values):
    square = values * values
    return square / (square + 2.0 * (1.0 - values) ** 2)


def following(values, along):
    count = values.shape[along]
    inner = lax.slice_in_dim(values, 1, count, axis=along)
    zeros = jnp.zeros_like(lax.slice_in_dim(values, 0, 1, axis=along))
    return jnp.concatenate([inner, zeros], axis=along)


def preceding(values, along):
    count = values.shape[along]
    inner = lax.slice_in_dim(values, 0, count - 1, axis=along)
    zeros = jnp.zeros_like(lax.slice_in_dim(values, 0, 1, axis=along))
    return jnp.concatenate([zeros, inner], axis=along)


def face_flux(velocity, here, there):
    return jnp.maximum(velocity, 0.0) * here + jnp.minimum(velocity, 0.0) * there


def last_face_closed(velocity, along, offset, total):
    positions = offset + lax.broadcasted_iota(jnp.int32, velocity.shape, along)
    return jnp.where(positions < total - 1, velocity, jnp.zeros_like(velocity))


def well_sources(flow_flat, cells, opened):
    terms = jnp.maximum(opened, 0.0) + jnp.minimum(opened, 0.0) * flow_flat[cells]
    return jnp.zeros_like(flow_flat).at[cells].add(terms)


def local(
    start_states,
    initial_state,
    x_velocity,
    y_velocity,
    z_velocity,
    step_scale,
    well_cells,
    well_rates,
    roster,
):
    width = x_velocity.shape[0]
    slab_number = lax.axis_index("gx")
    total_x = width * lax.axis_size("gx")
    x_closed = last_face_closed(x_velocity, 0, slab_number * width, total_x)
    z_closed = last_face_closed(z_velocity, 1, 0, z_velocity.shape[1])
    y_closed = last_face_closed(y_velocity, 2, 0, y_velocity.shape[2])
    opened = well_rates[0] * roster[0, 0].astype(jnp.float32)
    cells = well_cells[0]
    saturation = start_states[0]
    inflow = passed_along(x_closed[width - 1 :], "gx", 1)
    for turn in range(STEPS):
        extended = extended_2(saturation, (("gx", 0),), 1)
        flow_wide = fraction(extended)
        flow = flow_wide[1 : width + 1]
        x_face = face_flux(x_closed, flow, flow_wide[2:])
        entering = face_flux(inflow, flow_wide[0:1], flow_wide[1:2])
        z_face = face_flux(z_closed, flow, following(flow, 1))
        y_face = face_flux(y_closed, flow, following(flow, 2))
        outflow = (
            x_face
            - jnp.concatenate([entering, x_face[: width - 1]], axis=0)
            + (z_face - preceding(z_face, 1))
            + (y_face - preceding(y_face, 2))
        )
        sources = well_sources(flow.reshape(-1), cells, opened).reshape(flow.shape)
        saturation = saturation + step_scale * (sources - outflow)
    previous = passed_along(saturation, "shoot", 1)
    previous = jnp.where(lax.axis_index("shoot") == 0, initial_state, previous)
    defects = start_states[0] - previous
    return (saturation[None], defects[None])


def solution(mesh):
    placed = (
        P("shoot", "gx", None, None),
        P("gx", None, None),
        P("gx", None, None),
        P("gx", None, None),
        P("gx", None, None),
        P("gx", None, None),
        P("gx", None),
        P("gx", None),
        P("shoot", "gx", None),
    )
    return jax.shard_map(
        local,
        mesh=mesh,
        in_specs=placed,
        out_specs=(P("shoot", "gx", None, None), P("shoot", "gx", None, None)),
        check_vma=False,
    )
```

profile of v0, /device:TPU:20, one launch (start us, length us, event | category | flops | bytes accessed | tf_op | source)
XLA Modules:
  0.0 195.6 jit_solution(17855036152658655792)
XLA Ops:
  1.4 1.9 collective-permute-start.1
  3.3 2.4 %collective-permute-start = (f32[1,64,128]{2,1,0:T(8,128)S(1)}, f32[1,64,128]{2,1,0:T(8,128)S(1)}, u32[]{:S(2)}, u32[]{:S(2)}) collective-permute-start(f32[1,64,128]{2,1,0:T(8,128)S(1)} %get-tuple-element.54), channel_id=1, source_target_pairs={{0,1},{1,2},{2,3},{3,4},{4,5},{5,6},{6,7},{8,9},{9,10},{10,11},{11... | collective-permute-start | bytes 98312 | tf_op jit(solution)/shard_map/ppermute | solution.py:20
  6.5 2.1 %collective-permute-done = f32[1,64,128]{2,1,0:T(8,128)S(1)} collective-permute-done((f32[1,64,128]{2,1,0:T(8,128)S(1)}, f32[1,64,128]{2,1,0:T(8,128)S(1)}, u32[]{:S(2)}, u32[]{:S(2)}) %collective-permute-start) | collective-permute-done | bytes 32800 | tf_op jit(solution)/shard_map/ppermute | solution.py:20
  8.6 1.5 add_divide_fusion.7
  12.3 2.5 %multiply_add_fusion.15 = (f32[32,64,128]{2,1,0:T(8,128)}, f32[32,64,128]{2,1,0:T(8,128)}, f32[32,64,128]{2,1,0:T(8,128)}, f32[32,64,128]{2,1,0:T(8,128)S(1)}, f32[32,64,128]{2,1,0:T(8,128)}) fusion(f32[32,63,128]{2,1,0:T(8,128)S(1)} %slice.402, f32[34,64,128]{2,1,0:T(8,128)S(1)} %add_divide_fusion.7, f32[32,64,128]{2,1,0:T(8,128)S(1)} %copy-done.1, ...), kind=kLoop, calls=%fused_computation.112 | loop fusion | flops 4718592 | bytes 12558560 | tf_op jit(solution)/shard_map/add | solution.py:48
  14.8 1.9 collective-permute-start.2
  16.7 1.4 gather_fusion
  18.2 2.3 %slice.401 = f32[31,64,128]{2,1,0:T(8,128)} slice(f32[32,64,128]{2,1,0:T(8,128)} %get-tuple-element.37), slice={[0:31], [0:64], [0:128]} | slice | bytes 2031616 | tf_op jit(solution)/shard_map/slice | solution.py:92
  20.5 1.7 scatter_custom_fusion
  23.0 4.9 %fusion.12 = f32[32,64,128]{2,1,0:T(8,128)S(1)} fusion(f32[32,64,128]{2,1,0:T(8,128)} %param.14, f32[32,64,128]{2,1,0:T(8,128)} %bitcast.79, f32[32,64,128]{2,1,0:T(8,128)} %get-tuple-element.37, f32[31,64,128]{2,1,0:T(8,128)} %slice.401, f32[1,64,128]{2,1,0:T(8,128)S(1)} %fusion.71, f32[32,64,128]{2,1,0:T(8,128)} %get-tuple-element.36, ...), kind=kLoop, calls=%fused_computation.53 | loop fusion | flops 2359296 | bytes 10461184 | tf_op jit(solution)/shard_map/add | solution.py:97
  27.9 3.6 %collective-permute-start.4 = (f32[1,64,128]{2,1,0:T(8,128)S(1)}, f32[1,64,128]{2,1,0:T(8,128)S(1)}, u32[]{:S(2)}, u32[]{:S(2)}) collective-permute-start(f32[1,64,128]{2,1,0:T(8,128)S(1)} %get-tuple-element.53), channel_id=1, source_target_pairs={{1,0},{2,1},{3,2},{4,3},{5,4},{6,5},{7,6},{9,8},{10,9},{11,10},{12... | collective-permute-start | bytes 98312 | tf_op jit(solution)/shard_map/ppermute | solution.py:23
  31.5 1.9 collective-permute-start.3
  33.5 3.3 %collective-permute-done.3 = f32[1,64,128]{2,1,0:T(8,128)S(1)} collective-permute-done((f32[1,64,128]{2,1,0:T(8,128)S(1)}, f32[1,64,128]{2,1,0:T(8,128)S(1)}, u32[]{:S(2)}, u32[]{:S(2)}) %collective-permute-start.3) | collective-permute-done | bytes 32800 | tf_op jit(solution)/shard_map/ppermute | solution.py:20
  38.0 2.4 %multiply_add_fusion.13 = (f32[32,64,128]{2,1,0:T(8,128)}, f32[32,64,128]{2,1,0:T(8,128)}, f32[32,64,128]{2,1,0:T(8,128)}, f32[32,64,128]{2,1,0:T(8,128)}) fusion(f32[32,63,128]{2,1,0:T(8,128)S(1)} %slice.413, f32[34,64,128]{2,1,0:T(8,128)S(1)} %add_divide_fusion.6, f32[32,64,128]{2,1,0:T(8,128)S(1)} %copy-done.1, pred[64]{0:T(512)(128)(4,1)S(1)} %iota_compare_fusion.1, ...), kind=kLoop, calls=%fused_computation.110 | loop fusion | flops 4456448 | bytes 11509952 | tf_op jit(solution)/shard_map/add | solution.py:48
  40.5 1.4 gather_fusion.1
  42.9 1.5 slice.412
  45.1 2.9 %fusion.17 = f32[32,64,128]{2,1,0:T(8,128)S(1)} fusion(f32[32,64,128]{2,1,0:T(8,128)S(1)} %copy-done.8, f32[32,64,128]{2,1,0:T(8,128)S(1)} %copy-done.3, f32[32,64,128]{2,1,0:T(8,128)S(1)} %bitcast.81, f32[32,64,128]{2,1,0:T(8,128)} %get-tuple-element.33, f32[31,64,128]{2,1,0:T(8,128)S(1)} %slice.412, f32[1,64,128]{2,1,0:T(8,128)S(1)} %fusion.70, ...), kind=kLoop, calls=%fused_computation.59 | loop fusion | flops 2359296 | bytes 10461184 | tf_op jit(solution)/shard_map/add | solution.py:97
  48.1 1.9 collective-permute-start.6
  50.0 2.4 %collective-permute-start.5 = (f32[1,64,128]{2,1,0:T(8,128)S(1)}, f32[1,64,128]{2,1,0:T(8,128)S(1)}, u32[]{:S(2)}, u32[]{:S(2)}) collective-permute-start(f32[1,64,128]{2,1,0:T(8,128)S(1)} %get-tuple-element.50), channel_id=1, source_target_pairs={{0,1},{1,2},{2,3},{3,4},{4,5},{5,6},{6,7},{8,9},{9,10},{10,11},{11... | collective-permute-start | bytes 98312 | tf_op jit(solution)/shard_map/ppermute | solution.py:20
  52.4 2.8 %collective-permute-done.5 = f32[1,64,128]{2,1,0:T(8,128)S(1)} collective-permute-done((f32[1,64,128]{2,1,0:T(8,128)S(1)}, f32[1,64,128]{2,1,0:T(8,128)S(1)}, u32[]{:S(2)}, u32[]{:S(2)}) %collective-permute-start.5) | collective-permute-done | bytes 32800 | tf_op jit(solution)/shard_map/ppermute | solution.py:20
  55.9 3.8 %multiply_add_fusion.11 = (f32[32,64,128]{2,1,0:T(8,128)S(1)}, f32[32,64,128]{2,1,0:T(8,128)}, f32[32,64,128]{2,1,0:T(8,128)}, f32[32,64,128]{2,1,0:T(8,128)}) fusion(f32[32,63,128]{2,1,0:T(8,128)S(1)} %slice.424, f32[34,64,128]{2,1,0:T(8,128)S(1)} %add_divide_fusion.5, f32[32,64,128]{2,1,0:T(8,128)} %param.13, pred[64]{0:T(512)(128)(4,1)S(1)} %iota_compare_fusion.1, ...), kind=kLoop, calls=%fused_computation.108 | loop fusion | flops 4456448 | bytes 11509952 | tf_op jit(solution)/shard_map/add | solution.py:48
  59.8 1.5 gather_fusion.2
  61.3 1.8 scatter_custom_fusion.2
  63.1 1.4 slice.423
  64.7 2.9 %fusion.22 = f32[32,64,128]{2,1,0:T(8,128)S(1)} fusion(f32[32,64,128]{2,1,0:T(8,128)S(1)} %fusion.17, f32[32,64,128]{2,1,0:T(8,128)} %param.14, f32[32,64,128]{2,1,0:T(8,128)} %bitcast.82, f32[32,64,128]{2,1,0:T(8,128)} %get-tuple-element.29, f32[31,64,128]{2,1,0:T(8,128)S(1)} %slice.423, f32[1,64,128]{2,1,0:T(8,128)S(1)} %fusion.69, ...), kind=kLoop, calls=%fused_computation.65 | loop fusion | flops 2359296 | bytes 10461184 | tf_op jit(solution)/shard_map/add | solution.py:97
  67.6 1.9 collective-permute-start.8
  69.5 2.6 %collective-permute-start.7 = (f32[1,64,128]{2,1,0:T(8,128)S(1)}, f32[1,64,128]{2,1,0:T(8,128)S(1)}, u32[]{:S(2)}, u32[]{:S(2)}) collective-permute-start(f32[1,64,128]{2,1,0:T(8,128)S(1)} %get-tuple-element.48), channel_id=1, source_target_pairs={{0,1},{1,2},{2,3},{3,4},{4,5},{5,6},{6,7},{8,9},{9,10},{10,11},{11... | collective-permute-start | bytes 98312 | tf_op jit(solution)/shard_map/ppermute | solution.py:20
  72.1 2.6 %collective-permute-done.7 = f32[1,64,128]{2,1,0:T(8,128)S(1)} collective-permute-done((f32[1,64,128]{2,1,0:T(8,128)S(1)}, f32[1,64,128]{2,1,0:T(8,128)S(1)}, u32[]{:S(2)}, u32[]{:S(2)}) %collective-permute-start.7) | collective-permute-done | bytes 32800 | tf_op jit(solution)/shard_map/ppermute | solution.py:20
  75.5 4.2 %multiply_add_fusion.9 = (f32[32,64,128]{2,1,0:T(8,128)}, f32[32,64,128]{2,1,0:T(8,128)}, f32[32,64,128]{2,1,0:T(8,128)}, f32[32,64,128]{2,1,0:T(8,128)}) fusion(f32[32,63,128]{2,1,0:T(8,128)S(1)} %slice.435, f32[34,64,128]{2,1,0:T(8,128)S(1)} %add_divide_fusion.4, f32[32,64,128]{2,1,0:T(8,128)} %param.13, pred[64]{0:T(512)(128)(4,1)S(1)} %iota_compare_fusion.1, ...), kind=kLoop, calls=%fused_computation.106 | loop fusion | flops 4456448 | bytes 11509952 | tf_op jit(solution)/shard_map/add | solution.py:48
  79.7 1.5 gather_fusion.3
  81.2 1.8 scatter_custom_fusion.3
  83.0 1.5 slice.434
  84.9 2.9 %fusion.27 = f32[32,64,128]{2,1,0:T(8,128)S(1)} fusion(f32[32,64,128]{2,1,0:T(8,128)S(1)} %fusion.22, f32[32,64,128]{2,1,0:T(8,128)} %param.14, f32[32,64,128]{2,1,0:T(8,128)} %bitcast.83, f32[32,64,128]{2,1,0:T(8,128)} %get-tuple-element.25, f32[31,64,128]{2,1,0:T(8,128)S(1)} %slice.434, f32[1,64,128]{2,1,0:T(8,128)S(1)} %fusion.68, ...), kind=kLoop, calls=%fused_computation.71 | loop fusion | flops 2359296 | bytes 10461184 | tf_op jit(solution)/shard_map/add | solution.py:97
  87.8 1.9 collective-permute-start.10
  89.7 2.4 %collective-permute-start.9 = (f32[1,64,128]{2,1,0:T(8,128)S(1)}, f32[1,64,128]{2,1,0:T(8,128)S(1)}, u32[]{:S(2)}, u32[]{:S(2)}) collective-permute-start(f32[1,64,128]{2,1,0:T(8,128)S(1)} %get-tuple-element.46), channel_id=1, source_target_pairs={{0,1},{1,2},{2,3},{3,4},{4,5},{5,6},{6,7},{8,9},{9,10},{10,11},{11... | collective-permute-start | bytes 98312 | tf_op jit(solution)/shard_map/ppermute | solution.py:20
  92.2 2.8 %collective-permute-done.9 = f32[1,64,128]{2,1,0:T(8,128)S(1)} collective-permute-done((f32[1,64,128]{2,1,0:T(8,128)S(1)}, f32[1,64,128]{2,1,0:T(8,128)S(1)}, u32[]{:S(2)}, u32[]{:S(2)}) %collective-permute-start.9) | collective-permute-done | bytes 32800 | tf_op jit(solution)/shard_map/ppermute | solution.py:20
  95.7 3.8 %multiply_add_fusion.7 = (f32[32,64,128]{2,1,0:T(8,128)S(1)}, f32[32,64,128]{2,1,0:T(8,128)}, f32[32,64,128]{2,1,0:T(8,128)}, f32[32,64,128]{2,1,0:T(8,128)}) fusion(f32[32,63,128]{2,1,0:T(8,128)S(1)} %slice.446, f32[34,64,128]{2,1,0:T(8,128)S(1)} %add_divide_fusion.3, f32[32,64,128]{2,1,0:T(8,128)} %param.13, pred[64]{0:T(512)(128)(4,1)S(1)} %iota_compare_fusion.1, ...), kind=kLoop, calls=%fused_computation.104 | loop fusion | flops 4456448 | bytes 11509952 | tf_op jit(solution)/shard_map/add | solution.py:48
  99.5 1.5 gather_fusion.4
  101.0 1.8 scatter_custom_fusion.4
  102.8 1.4 slice.445
  104.4 2.9 %fusion.32 = f32[32,64,128]{2,1,0:T(8,128)S(1)} fusion(f32[32,64,128]{2,1,0:T(8,128)S(1)} %fusion.27, f32[32,64,128]{2,1,0:T(8,128)} %param.14, f32[32,64,128]{2,1,0:T(8,128)} %bitcast.84, f32[32,64,128]{2,1,0:T(8,128)} %get-tuple-element.21, f32[31,64,128]{2,1,0:T(8,128)S(1)} %slice.445, f32[1,64,128]{2,1,0:T(8,128)S(1)} %fusion.67, ...), kind=kLoop, calls=%fused_computation.77 | loop fusion | flops 2359296 | bytes 10461184 | tf_op jit(solution)/shard_map/add | solution.py:97
  107.3 1.9 collective-permute-start.12
  109.2 2.4 %collective-permute-start.11 = (f32[1,64,128]{2,1,0:T(8,128)S(1)}, f32[1,64,128]{2,1,0:T(8,128)S(1)}, u32[]{:S(2)}, u32[]{:S(2)}) collective-permute-start(f32[1,64,128]{2,1,0:T(8,128)S(1)} %get-tuple-element.44), channel_id=1, source_target_pairs={{0,1},{1,2},{2,3},{3,4},{4,5},{5,6},{6,7},{8,9},{9,10},{10,11},{11... | collective-permute-start | bytes 98312 | tf_op jit(solution)/shard_map/ppermute | solution.py:20
  111.7 2.8 %collective-permute-done.11 = f32[1,64,128]{2,1,0:T(8,128)S(1)} collective-permute-done((f32[1,64,128]{2,1,0:T(8,128)S(1)}, f32[1,64,128]{2,1,0:T(8,128)S(1)}, u32[]{:S(2)}, u32[]{:S(2)}) %collective-permute-start.11) | collective-permute-done | bytes 32800 | tf_op jit(solution)/shard_map/ppermute | solution.py:20
  115.2 3.8 %multiply_add_fusion.5 = (f32[32,64,128]{2,1,0:T(8,128)S(1)}, f32[32,64,128]{2,1,0:T(8,128)}, f32[32,64,128]{2,1,0:T(8,128)}, f32[32,64,128]{2,1,0:T(8,128)}) fusion(f32[32,63,128]{2,1,0:T(8,128)S(1)} %slice.457, f32[34,64,128]{2,1,0:T(8,128)S(1)} %add_divide_fusion.2, f32[32,64,128]{2,1,0:T(8,128)} %param.13, pred[64]{0:T(512)(128)(4,1)S(1)} %iota_compare_fusion.1, ...), kind=kLoop, calls=%fused_computation.102 | loop fusion | flops 4456448 | bytes 11509952 | tf_op jit(solution)/shard_map/add | solution.py:48
  119.0 1.5 gather_fusion.5
  120.6 1.8 scatter_custom_fusion.5
  123.9 2.9 %fusion.37 = f32[32,64,128]{2,1,0:T(8,128)S(1)} fusion(f32[32,64,128]{2,1,0:T(8,128)S(1)} %fusion.32, f32[32,64,128]{2,1,0:T(8,128)} %param.14, f32[32,64,128]{2,1,0:T(8,128)} %bitcast.85, f32[32,64,128]{2,1,0:T(8,128)} %get-tuple-element.17, f32[31,64,128]{2,1,0:T(8,128)S(1)} %slice.456, f32[1,64,128]{2,1,0:T(8,128)S(1)} %fusion.66, ...), kind=kLoop, calls=%fused_computation.83 | loop fusion | flops 2359296 | bytes 10461184 | tf_op jit(solution)/shard_map/add | solution.py:97
  126.8 1.9 collective-permute-start.14
  128.8 2.4 %collective-permute-start.13 = (f32[1,64,128]{2,1,0:T(8,128)S(1)}, f32[1,64,128]{2,1,0:T(8,128)S(1)}, u32[]{:S(2)}, u32[]{:S(2)}) collective-permute-start(f32[1,64,128]{2,1,0:T(8,128)S(1)} %get-tuple-element.42), channel_id=1, source_target_pairs={{0,1},{1,2},{2,3},{3,4},{4,5},{5,6},{6,7},{8,9},{9,10},{10,11},{11... | collective-permute-start | bytes 98312 | tf_op jit(solution)/shard_map/ppermute | solution.py:20
  131.2 2.8 %collective-permute-done.13 = f32[1,64,128]{2,1,0:T(8,128)S(1)} collective-permute-done((f32[1,64,128]{2,1,0:T(8,128)S(1)}, f32[1,64,128]{2,1,0:T(8,128)S(1)}, u32[]{:S(2)}, u32[]{:S(2)}) %collective-permute-start.13) | collective-permute-done | bytes 32800 | tf_op jit(solution)/shard_map/ppermute | solution.py:20
  134.7 3.9 %multiply_add_fusion.3 = (f32[32,64,128]{2,1,0:T(8,128)S(1)}, f32[32,64,128]{2,1,0:T(8,128)S(1)}, f32[32,64,128]{2,1,0:T(8,128)}, f32[32,64,128]{2,1,0:T(8,128)}) fusion(f32[32,63,128]{2,1,0:T(8,128)S(1)} %slice.468, f32[34,64,128]{2,1,0:T(8,128)S(1)} %add_divide_fusion.1, f32[32,64,128]{2,1,0:T(8,128)} %param.13, pred[64]{0:T(512)(128)(4,1)S(1)} %iota_compare_fusion.1, ...), kind=kLoop, calls=%fused_computation.100 | loop fusion | flops 4456448 | bytes 11509952 | tf_op jit(solution)/shard_map/add | solution.py:48
  138.6 1.5 gather_fusion.6
  140.1 1.8 scatter_custom_fusion.6
  143.5 2.9 %fusion.42 = f32[32,64,128]{2,1,0:T(8,128)S(1)} fusion(f32[32,64,128]{2,1,0:T(8,128)S(1)} %copy-done.10, f32[32,64,128]{2,1,0:T(8,128)} %param.14, f32[32,64,128]{2,1,0:T(8,128)} %bitcast.86, f32[32,64,128]{2,1,0:T(8,128)} %get-tuple-element.13, f32[31,64,128]{2,1,0:T(8,128)S(1)} %slice.467, f32[1,64,128]{2,1,0:T(8,128)S(1)} %fusion.65, ...), kind=kLoop, calls=%fused_computation.89 | loop fusion | flops 2359296 | bytes 10461184 | tf_op jit(solution)/shard_map/add | solution.py:97
  146.4 1.9 collective-permute-start.16
  148.3 2.4 %collective-permute-start.15 = (f32[1,64,128]{2,1,0:T(8,128)S(1)}, f32[1,64,128]{2,1,0:T(8,128)S(1)}, u32[]{:S(2)}, u32[]{:S(2)}) collective-permute-start(f32[1,64,128]{2,1,0:T(8,128)S(1)} %get-tuple-element.40), channel_id=1, source_target_pairs={{0,1},{1,2},{2,3},{3,4},{4,5},{5,6},{6,7},{8,9},{9,10},{10,11},{11... | collective-permute-start | bytes 98312 | tf_op jit(solution)/shard_map/ppermute | solution.py:20
  150.8 2.8 %collective-permute-done.15 = f32[1,64,128]{2,1,0:T(8,128)S(1)} collective-permute-done((f32[1,64,128]{2,1,0:T(8,128)S(1)}, f32[1,64,128]{2,1,0:T(8,128)S(1)}, u32[]{:S(2)}, u32[]{:S(2)}) %collective-permute-start.15) | collective-permute-done | bytes 32800 | tf_op jit(solution)/shard_map/ppermute | solution.py:20
  154.3 3.8 %multiply_add_fusion.1 = (f32[32,64,128]{2,1,0:T(8,128)S(1)}, f32[32,64,128]{2,1,0:T(8,128)}, f32[32,64,128]{2,1,0:T(8,128)}, f32[32,64,128]{2,1,0:T(8,128)}) fusion(f32[32,63,128]{2,1,0:T(8,128)S(1)} %slice.479, f32[34,64,128]{2,1,0:T(8,128)S(1)} %add_divide_fusion, f32[32,64,128]{2,1,0:T(8,128)} %param.13, pred[64]{0:T(512)(128)(4,1)S(1)} %iota_compare_fusion.1, ...), kind=kLoop, calls=%fused_computation.98 | loop fusion | flops 4456448 | bytes 11509952 | tf_op jit(solution)/shard_map/add | solution.py:48
  158.1 1.5 gather_fusion.7
  159.6 1.8 scatter_custom_fusion.7
  163.0 4.0 %fusion.47 = f32[32,64,128]{2,1,0:T(8,128)} fusion(f32[32,64,128]{2,1,0:T(8,128)S(1)} %fusion.42, f32[32,64,128]{2,1,0:T(8,128)} %param.14, f32[32,64,128]{2,1,0:T(8,128)} %bitcast.80, f32[32,64,128]{2,1,0:T(8,128)} %get-tuple-element.9, f32[31,64,128]{2,1,0:T(8,128)S(1)} %slice.478, f32[1,64,128]{2,1,0:T(8,128)S(1)} %fusion.64, ...), kind=kLoop, calls=%fused_computation.95 | loop fusion | flops 2359296 | bytes 10461184 | tf_op jit(solution)/shard_map/add | solution.py:97
  167.0 3.4 %collective-permute-start.17 = (f32[32,64,128]{2,1,0:T(8,128)}, f32[32,64,128]{2,1,0:T(8,128)S(1)}, u32[]{:S(2)}, u32[]{:S(2)}) collective-permute-start(f32[32,64,128]{2,1,0:T(8,128)} %fusion.47), channel_id=1, source_target_pairs={{0,8},{8,16},{16,24},{1,9},{9,17},{17,25},{2,10},{10,18},{18,26},{... | collective-permute-start | bytes 3145736 | tf_op jit(solution)/shard_map/ppermute | solution.py:12
  170.4 24.0 %collective-permute-done.17 = f32[32,64,128]{2,1,0:T(8,128)S(1)} collective-permute-done((f32[32,64,128]{2,1,0:T(8,128)}, f32[32,64,128]{2,1,0:T(8,128)S(1)}, u32[]{:S(2)}, u32[]{:S(2)}) %collective-permute-start.17) | collective-permute-done | bytes 1048608 | tf_op jit(solution)/shard_map/ppermute | solution.py:12
  (113 shorter events, 18.1 us)
Async XLA Ops:
  1.4 5.1 %collective-permute-start.1 = (f32[1,64,128]{2,1,0:T(8,128)S(1)}, f32[1,64,128]{2,1,0:T(8,128)S(1)}, u32[]{:S(2)}, u32[]{:S(2)}) collective-permute-start(f32[1,64,128]{2,1,0:T(8,128)S(1)} %get-tuple-element.55), channel_id=1, source_target_pairs={{1,0},{2,1},{3,2},{4,3},{5,4},{6,5},{7,6},{9,8},{10,9},{11,10},{12... | collective-permute-start | bytes 98312 | tf_op jit(solution)/shard_map/ppermute | solution.py:23
  3.3 5.2 %collective-permute-start = (f32[1,64,128]{2,1,0:T(8,128)S(1)}, f32[1,64,128]{2,1,0:T(8,128)S(1)}, u32[]{:S(2)}, u32[]{:S(2)}) collective-permute-start(f32[1,64,128]{2,1,0:T(8,128)S(1)} %get-tuple-element.54), channel_id=1, source_target_pairs={{0,1},{1,2},{2,3},{3,4},{4,5},{5,6},{6,7},{8,9},{9,10},{10,11},{11... | collective-permute-start | bytes 98312 | tf_op jit(solution)/shard_map/ppermute | solution.py:20
  6.4 35.4 %copy-start.20 = (s32[16]{0:T(128)}, s32[16]{0:T(128)S(1)}, u32[]{:S(2)}) copy-start(s32[16]{0:T(128)S(1)} %fusion.72) | copy-start | bytes 196
  6.4 34.0 %copy-start.19 = (s32[1024]{0:T(1024)}, s32[1024]{0:T(1024)S(1)}, u32[]{:S(2)}) copy-start(s32[1024]{0:T(1024)S(1)} %pad_clamp_fusion) | copy-start | bytes 12292
  10.1 1.0 copy-start.4
  10.1 1.6 copy-start.18
  10.2 1.8 copy-start.1
  10.2 2.1 %copy-start.2 = (f32[32,64,128]{2,1,0:T(8,128)S(1)}, f32[32,64,128]{2,1,0:T(8,128)}, u32[]{:S(2)}) copy-start(f32[32,64,128]{2,1,0:T(8,128)} %param.12) | copy-start | bytes 3145732
  12.3 5.8 %copy-start.21 = (s32[1,1,16]{2,1,0:T(1,128)S(1)}, s32[1,1,16]{2,1,0:T(1,128)}, u32[]{:S(2)}) copy-start(s32[1,1,16]{2,1,0:T(1,128)} %param.17) | copy-start | bytes 196
  12.3 5.8 %copy-start.22 = (f32[1,16]{1,0:T(1,128)S(1)}, f32[1,16]{1,0:T(1,128)}, u32[]{:S(2)}) copy-start(f32[1,16]{1,0:T(1,128)} %param.16) | copy-start | bytes 196
  14.8 22.7 %copy-start = (f32[32,64,128]{2,1,0:T(8,128)}, f32[32,64,128]{2,1,0:T(8,128)S(1)}, u32[]{:S(2)}) copy-start(f32[32,64,128]{2,1,0:T(8,128)S(1)} %get-tuple-element.38) | copy-start | bytes 3145732
  14.8 7.4 %collective-permute-start.2 = (f32[1,64,128]{2,1,0:T(8,128)S(1)}, f32[1,64,128]{2,1,0:T(8,128)S(1)}, u32[]{:S(2)}, u32[]{:S(2)}) collective-permute-start(f32[1,64,128]{2,1,0:T(8,128)S(1)} %slice.398), channel_id=1, source_target_pairs={{0,1},{1,2},{2,3},{3,4},{4,5},{5,6},{6,7},{8,9},{9,10},{10,11},{11... | collective-permute-start | bytes 98312 | tf_op jit(solution)/shard_map/ppermute | solution.py:12
  27.9 9.2 %copy-start.7 = (f32[32,64,128]{2,1,0:T(8,128)}, f32[32,64,128]{2,1,0:T(8,128)S(1)}, u32[]{:S(2)}) copy-start(f32[32,64,128]{2,1,0:T(8,128)S(1)} %fusion.12) | copy-start | bytes 3145732
  27.9 5.6 %collective-permute-start.4 = (f32[1,64,128]{2,1,0:T(8,128)S(1)}, f32[1,64,128]{2,1,0:T(8,128)S(1)}, u32[]{:S(2)}, u32[]{:S(2)}) collective-permute-start(f32[1,64,128]{2,1,0:T(8,128)S(1)} %get-tuple-element.53), channel_id=1, source_target_pairs={{1,0},{2,1},{3,2},{4,3},{5,4},{6,5},{7,6},{9,8},{10,9},{11,10},{12... | collective-permute-start | bytes 98312 | tf_op jit(solution)/shard_map/ppermute | solution.py:23
  31.5 5.2 %collective-permute-start.3 = (f32[1,64,128]{2,1,0:T(8,128)S(1)}, f32[1,64,128]{2,1,0:T(8,128)S(1)}, u32[]{:S(2)}, u32[]{:S(2)}) collective-permute-start(f32[1,64,128]{2,1,0:T(8,128)S(1)} %get-tuple-element.52), channel_id=1, source_target_pairs={{0,1},{1,2},{2,3},{3,4},{4,5},{5,6},{6,7},{8,9},{9,10},{10,11},{11... | collective-permute-start | bytes 98312 | tf_op jit(solution)/shard_map/ppermute | solution.py:20
  37.0 1.0 copy-start.5
  41.9 3.2 %copy-start.12 = (f32[32,64,128]{2,1,0:T(8,128)S(1)}, f32[32,64,128]{2,1,0:T(8,128)}, u32[]{:S(2)}) copy-start(f32[32,64,128]{2,1,0:T(8,128)} %get-tuple-element.31) | copy-start | bytes 3145732
  42.8 2.3 %copy-start.3 = (f32[32,64,128]{2,1,0:T(8,128)S(1)}, f32[32,64,128]{2,1,0:T(8,128)}, u32[]{:S(2)}) copy-start(f32[32,64,128]{2,1,0:T(8,128)} %param.14) | copy-start | bytes 3145732
  42.8 2.3 %copy-start.8 = (f32[32,64,128]{2,1,0:T(8,128)S(1)}, f32[32,64,128]{2,1,0:T(8,128)}, u32[]{:S(2)}) copy-start(f32[32,64,128]{2,1,0:T(8,128)} %copy-done.7) | copy-start | bytes 3145732
  48.1 4.3 %collective-permute-start.6 = (f32[1,64,128]{2,1,0:T(8,128)S(1)}, f32[1,64,128]{2,1,0:T(8,128)S(1)}, u32[]{:S(2)}, u32[]{:S(2)}) collective-permute-start(f32[1,64,128]{2,1,0:T(8,128)S(1)} %get-tuple-element.51), channel_id=1, source_target_pairs={{1,0},{2,1},{3,2},{4,3},{5,4},{6,5},{7,6},{9,8},{10,9},{11,10},{12... | collective-permute-start | bytes 98312 | tf_op jit(solution)/shard_map/ppermute | solution.py:23
  50.0 5.2 %collective-permute-start.5 = (f32[1,64,128]{2,1,0:T(8,128)S(1)}, f32[1,64,128]{2,1,0:T(8,128)S(1)}, u32[]{:S(2)}, u32[]{:S(2)}) collective-permute-start(f32[1,64,128]{2,1,0:T(8,128)S(1)} %get-tuple-element.50), channel_id=1, source_target_pairs={{0,1},{1,2},{2,3},{3,4},{4,5},{5,6},{6,7},{8,9},{9,10},{10,11},{11... | collective-permute-start | bytes 98312 | tf_op jit(solution)/shard_map/ppermute | solution.py:20
  63.1 1.5 copy-start.13
  67.6 4.5 %collective-permute-start.8 = (f32[1,64,128]{2,1,0:T(8,128)S(1)}, f32[1,64,128]{2,1,0:T(8,128)S(1)}, u32[]{:S(2)}, u32[]{:S(2)}) collective-permute-start(f32[1,64,128]{2,1,0:T(8,128)S(1)} %get-tuple-element.49), channel_id=1, source_target_pairs={{1,0},{2,1},{3,2},{4,3},{5,4},{6,5},{7,6},{9,8},{10,9},{11,10},{12... | collective-permute-start | bytes 98312 | tf_op jit(solution)/shard_map/ppermute | solution.py:23
  69.5 5.2 %collective-permute-start.7 = (f32[1,64,128]{2,1,0:T(8,128)S(1)}, f32[1,64,128]{2,1,0:T(8,128)S(1)}, u32[]{:S(2)}, u32[]{:S(2)}) collective-permute-start(f32[1,64,128]{2,1,0:T(8,128)S(1)} %get-tuple-element.48), channel_id=1, source_target_pairs={{0,1},{1,2},{2,3},{3,4},{4,5},{5,6},{6,7},{8,9},{9,10},{10,11},{11... | collective-permute-start | bytes 98312 | tf_op jit(solution)/shard_map/ppermute | solution.py:20
  83.0 1.5 copy-start.14
  83.0 1.8 copy-start.15
  87.8 4.3 %collective-permute-start.10 = (f32[1,64,128]{2,1,0:T(8,128)S(1)}, f32[1,64,128]{2,1,0:T(8,128)S(1)}, u32[]{:S(2)}, u32[]{:S(2)}) collective-permute-start(f32[1,64,128]{2,1,0:T(8,128)S(1)} %get-tuple-element.47), channel_id=1, source_target_pairs={{1,0},{2,1},{3,2},{4,3},{5,4},{6,5},{7,6},{9,8},{10,9},{11,10},{12... | collective-permute-start | bytes 98312 | tf_op jit(solution)/shard_map/ppermute | solution.py:23
  89.7 5.2 %collective-permute-start.9 = (f32[1,64,128]{2,1,0:T(8,128)S(1)}, f32[1,64,128]{2,1,0:T(8,128)S(1)}, u32[]{:S(2)}, u32[]{:S(2)}) collective-permute-start(f32[1,64,128]{2,1,0:T(8,128)S(1)} %get-tuple-element.46), channel_id=1, source_target_pairs={{0,1},{1,2},{2,3},{3,4},{4,5},{5,6},{6,7},{8,9},{9,10},{10,11},{11... | collective-permute-start | bytes 98312 | tf_op jit(solution)/shard_map/ppermute | solution.py:20
  102.8 1.5 copy-start.16
  107.3 4.3 %collective-permute-start.12 = (f32[1,64,128]{2,1,0:T(8,128)S(1)}, f32[1,64,128]{2,1,0:T(8,128)S(1)}, u32[]{:S(2)}, u32[]{:S(2)}) collective-permute-start(f32[1,64,128]{2,1,0:T(8,128)S(1)} %get-tuple-element.45), channel_id=1, source_target_pairs={{1,0},{2,1},{3,2},{4,3},{5,4},{6,5},{7,6},{9,8},{10,9},{11,10},{12... | collective-permute-start | bytes 98312 | tf_op jit(solution)/shard_map/ppermute | solution.py:23
  109.2 5.2 %collective-permute-start.11 = (f32[1,64,128]{2,1,0:T(8,128)S(1)}, f32[1,64,128]{2,1,0:T(8,128)S(1)}, u32[]{:S(2)}, u32[]{:S(2)}) collective-permute-start(f32[1,64,128]{2,1,0:T(8,128)S(1)} %get-tuple-element.44), channel_id=1, source_target_pairs={{0,1},{1,2},{2,3},{3,4},{4,5},{5,6},{6,7},{8,9},{9,10},{10,11},{11... | collective-permute-start | bytes 98312 | tf_op jit(solution)/shard_map/ppermute | solution.py:20
  122.4 1.5 copy-start.17
  126.8 7.5 %copy-start.9 = (f32[32,64,128]{2,1,0:T(8,128)}, f32[32,64,128]{2,1,0:T(8,128)S(1)}, u32[]{:S(2)}) copy-start(f32[32,64,128]{2,1,0:T(8,128)S(1)} %fusion.37) | copy-start | bytes 3145732
  126.8 4.3 %collective-permute-start.14 = (f32[1,64,128]{2,1,0:T(8,128)S(1)}, f32[1,64,128]{2,1,0:T(8,128)S(1)}, u32[]{:S(2)}, u32[]{:S(2)}) collective-permute-start(f32[1,64,128]{2,1,0:T(8,128)S(1)} %get-tuple-element.43), channel_id=1, source_target_pairs={{1,0},{2,1},{3,2},{4,3},{5,4},{6,5},{7,6},{9,8},{10,9},{11,10},{12... | collective-permute-start | bytes 98312 | tf_op jit(solution)/shard_map/ppermute | solution.py:23
  128.8 5.2 %collective-permute-start.13 = (f32[1,64,128]{2,1,0:T(8,128)S(1)}, f32[1,64,128]{2,1,0:T(8,128)S(1)}, u32[]{:S(2)}, u32[]{:S(2)}) collective-permute-start(f32[1,64,128]{2,1,0:T(8,128)S(1)} %get-tuple-element.42), channel_id=1, source_target_pairs={{0,1},{1,2},{2,3},{3,4},{4,5},{5,6},{6,7},{8,9},{9,10},{10,11},{11... | collective-permute-start | bytes 98312 | tf_op jit(solution)/shard_map/ppermute | solution.py:20
  141.9 1.5 copy-start.10
  146.4 4.3 %collective-permute-start.16 = (f32[1,64,128]{2,1,0:T(8,128)S(1)}, f32[1,64,128]{2,1,0:T(8,128)S(1)}, u32[]{:S(2)}, u32[]{:S(2)}) collective-permute-start(f32[1,64,128]{2,1,0:T(8,128)S(1)} %get-tuple-element.41), channel_id=1, source_target_pairs={{1,0},{2,1},{3,2},{4,3},{5,4},{6,5},{7,6},{9,8},{10,9},{11,10},{12... | collective-permute-start | bytes 98312 | tf_op jit(solution)/shard_map/ppermute | solution.py:23
  148.3 5.2 %collective-permute-start.15 = (f32[1,64,128]{2,1,0:T(8,128)S(1)}, f32[1,64,128]{2,1,0:T(8,128)S(1)}, u32[]{:S(2)}, u32[]{:S(2)}) collective-permute-start(f32[1,64,128]{2,1,0:T(8,128)S(1)} %get-tuple-element.40), channel_id=1, source_target_pairs={{0,1},{1,2},{2,3},{3,4},{4,5},{5,6},{6,7},{8,9},{9,10},{10,11},{11... | collective-permute-start | bytes 98312 | tf_op jit(solution)/shard_map/ppermute | solution.py:20
  161.4 1.5 copy-start.11
  163.0 31.3 %copy-start.6 = (f32[1,32,64,128]{3,2,1,0:T(8,128)S(1)}, f32[1,32,64,128]{3,2,1,0:T(8,128)}, u32[]{:S(2)}) copy-start(f32[1,32,64,128]{3,2,1,0:T(8,128)} %param.9) | copy-start | bytes 3145732
  167.0 27.4 %collective-permute-start.17 = (f32[32,64,128]{2,1,0:T(8,128)}, f32[32,64,128]{2,1,0:T(8,128)S(1)}, u32[]{:S(2)}, u32[]{:S(2)}) collective-permute-start(f32[32,64,128]{2,1,0:T(8,128)} %fusion.47), channel_id=1, source_target_pairs={{0,8},{8,16},{16,24},{1,9},{9,17},{17,25},{2,10},{10,18},{18,26},{... | collective-permute-start | bytes 3145736 | tf_op jit(solution)/shard_map/ppermute | solution.py:12
where the time goes:
time: 197 us; the launch traced here: 196 us
  other arithmetic  75.1 us (38%)
  waiting for transfers between devices  46 us (23%)
  starting transfers between devices  41.3 us (21%)
  local copies, waits for them, and re-layouts  31.8 us (16%)
    add x16, other arithmetic, face_flux(): jnp.maximum(velocity, 0.0) * here + jnp.minimum(velocity, 0.0) * there  30 us
    add x8, other arithmetic, local(): saturation = saturation + step_scale * (sources - outflow)  26.4 us
    ppermute x2, waiting for transfers between devices, passed_along(): return lax.ppermute(block, axis, route)  24 us
    ppermute x8, waiting for transfers between devices, extended_2(): lax.ppermute(lax.slice_in_dim(block, block.shape[dim] - width, None, axis...  22.1 us
    ppermute x8, starting transfers between devices, extended_2(): lax.ppermute(lax.slice_in_dim(block, block.shape[dim] - width, None, axis...  18.9 us
    ppermute x8, starting transfers between devices, extended_2(): lax.ppermute(lax.slice_in_dim(block, 0, width, axis=dim), axis, backward)  17.1 us
    scatter-add x8, other arithmetic, well_sources(): return jnp.zeros_like(flow_flat).at[cells].add(terms)  13.4 us
    slice x8, local copies, waits for them, and re-layouts, local(): x_face[:width - 1]  12.2 us
  transfers between devices with their start and end apart: 18, of which 9 were waited for; matrix products, arithmetic and copies ran while one was open for 3% of the time, Pallas kernels for 0%

commit v1 on v0

v1 whole, which is shorter than its diff:
```python
import functools

import jax
import jax.numpy as jnp
from jax import lax
from jax.experimental import pallas as pl
from jax.experimental.pallas import tpu as pltpu
from jax.sharding import PartitionSpec as P

STEPS = 8
MESH = pl.DeviceIdType.MESH
PAD = 8


def tripled_fraction(s):
    square = s * s
    below = square + (2.0 / 3.0 - (4.0 / 3.0) * s)
    guess = pl.reciprocal(below, approx=True)
    return (square * guess) * (2.0 - below * guess)


def kernel(
    nx, nz, ny,
    start_hbm, initial_hbm, ux_hbm, uy_hbm, uz_hbm, scale_hbm, cells_ref, rates_ref, roster_ref,
    ends_hbm, defects_hbm,
    start, ux, uy, uz, scale, s_odd, s_even, f_even, f_odd, coef, add_well, mul_well, received, raw,
    load_sem, out_sem, first_send, first_recv, halo_send, halo_recv, end_send, end_recv,
):
    k, g = lax.axis_index("shoot"), lax.axis_index("gx")
    intervals, slabs = lax.axis_size("shoot"), lax.axis_size("gx")
    has_left, has_right = g > 0, g < slabs - 1
    has_before, has_after = k > 0, k < intervals - 1
    left, right, after, before = (k, g - 1), (k, g + 1), (k + 1, g), (k - 1, g)
    last = nx - 1
    rows = nx * nz
    base = PAD + nz
    half = nx // 2

    def plane(p, offset=0, count=1):
        first = p * nz if isinstance(p, int) else pl.multiple_of(p * nz, nz)
        return pl.ds(first + offset, count * nz)

    loads = [
        pltpu.make_async_copy(start_hbm, start, load_sem.at[0]),
        pltpu.make_async_copy(ux_hbm, ux.at[pl.ds(nz, rows)], load_sem.at[1]),
        pltpu.make_async_copy(uz_hbm, uz.at[pl.ds(PAD, rows)], load_sem.at[2]),
        pltpu.make_async_copy(uy_hbm, uy, load_sem.at[3]),
        pltpu.make_async_copy(scale_hbm, scale, load_sem.at[4]),
    ]
    for load in loads:
        load.start()
    initial_load = pltpu.make_async_copy(initial_hbm, received, load_sem.at[5])

    @pl.when(jnp.logical_not(has_before))
    def _():
        initial_load.start()

    blank = jnp.zeros((nz, ny), jnp.float32)
    for ref in (f_even, f_odd):
        ref[0:PAD, :] = blank[:PAD]
        ref[rows + 2 * nz + PAD :, :] = blank[:PAD]

        @pl.loop(0, nx + 2)
        def _(p):
            ref[plane(p, PAD), :] = blank

    ux[0:nz, :] = blank
    uz[0:PAD, :] = blank[:PAD]
    raw[0] = blank
    raw[1] = blank

    barrier = pltpu.get_barrier_semaphore()
    for there, target in ((has_left, left), (has_right, right), (has_before, before)):

        @pl.when(there)
        def _():
            pl.semaphore_signal(barrier, 1, device_id=target, device_id_type=MESH)

    peers = has_left.astype(jnp.int32) + has_right.astype(jnp.int32) + has_after.astype(jnp.int32)
    pl.semaphore_wait(barrier, peers)

    def remote(source, target, send, recv, device):
        return pltpu.make_async_remote_copy(
            src_ref=source, dst_ref=target, send_sem=send, recv_sem=recv,
            device_id=device, device_id_type=MESH,
        )

    first_left = remote(start_hbm.at[plane(0)], raw.at[1], first_send.at[0], first_recv.at[0], left)
    first_right = remote(start_hbm.at[plane(last)], raw.at[0], first_send.at[1], first_recv.at[1], right)
    face_right = remote(ux_hbm.at[plane(last)], ux.at[pl.ds(0, nz)], first_send.at[2], first_recv.at[2], right)

    @pl.when(has_left)
    def _():
        first_left.start()

    @pl.when(has_right)
    def _():
        first_right.start()
        face_right.start()

    well_rows = (nx - 2 * STEPS) * nz
    slots = cells_ref.shape[1]
    cells = cells_ref[...]
    opened = rates_ref[...] * roster_ref[...].astype(jnp.float32)
    row_of = lax.broadcasted_iota(jnp.int32, (well_rows, slots), 0) + STEPS * nz
    in_row = jnp.where(row_of == lax.shift_right_logical(cells, ny.bit_length() - 1), 1.0, 0.0)
    column_of = lax.broadcasted_iota(jnp.int32, (ny, slots), 0)
    in_column = column_of == jnp.bitwise_and(cells, ny - 1)
    for well, part in ((add_well, jnp.maximum(opened, 0.0)), (mul_well, jnp.minimum(opened, 0.0))):
        well[pl.ds(0, STEPS * nz), :] = jnp.zeros((STEPS * nz, ny), jnp.float32)
        well[pl.ds(rows - STEPS * nz, STEPS * nz), :] = jnp.zeros((STEPS * nz, ny), jnp.float32)
        well[pl.ds(STEPS * nz, well_rows), :] = lax.dot_general(
            in_row, jnp.where(in_column, part, 0.0), (((1,), (1,)), ((), ())),
            precision=lax.Precision.HIGHEST, preferred_element_type=jnp.float32,
        )

    for load in loads:
        load.wait()

    z_of = lax.broadcasted_iota(jnp.int32, (nz, ny), 0)
    y_of = lax.broadcasted_iota(jnp.int32, (nz, ny), 1)

    def prepare(p):
        here = plane(p)
        f_even[plane(p, base), :] = tripled_fraction(start[here, :])
        h = scale[here, :]
        third = h * (1.0 / 3.0)
        closed = jnp.logical_and(jnp.logical_not(has_right), p == last)
        u = jnp.where(closed, 0.0, ux[plane(p, nz), :])
        v = ux[plane(p), :]
        total = jnp.maximum(u, 0.0) - jnp.minimum(v, 0.0)
        coef[1, here, :] = -third * jnp.minimum(u, 0.0)
        coef[2, here, :] = third * jnp.maximum(v, 0.0)
        u = jnp.where(z_of == nz - 1, 0.0, uz[plane(p, PAD), :])
        v = jnp.where(z_of == 0, 0.0, uz[plane(p, PAD - 1), :])
        total = total + (jnp.maximum(u, 0.0) - jnp.minimum(v, 0.0))
        coef[3, here, :] = -third * jnp.minimum(u, 0.0)
        coef[4, here, :] = third * jnp.maximum(v, 0.0)
        u = jnp.where(y_of == ny - 1, 0.0, uy[here, :])
        v = jnp.where(y_of == 0, 0.0, pltpu.roll(uy[here, :], 1, 1))
        total = total + (jnp.maximum(u, 0.0) - jnp.minimum(v, 0.0))
        coef[5, here, :] = -third * jnp.minimum(u, 0.0)
        coef[6, here, :] = third * jnp.maximum(v, 0.0)
        coef[0, here, :] = third * (mul_well[here, :] - total)
        coef[7, here, :] = h * add_well[here, :]

    def advance(p, t):
        here = plane(p)
        s_old = start if t == 1 else (s_even if t % 2 else s_odd)
        s_new = s_odd if t % 2 else s_even
        f_old, f_new = (f_even, f_odd) if t % 2 else (f_odd, f_even)
        f = f_old[plane(p, base), :]
        x = coef[1, here, :] * f_old[plane(p, base + nz), :] + coef[2, here, :] * f_old[plane(p, base - nz), :]
        z = coef[3, here, :] * f_old[plane(p, base + 1), :] + coef[4, here, :] * f_old[plane(p, base - 1), :]
        y = coef[5, here, :] * pltpu.roll(f, ny - 1, 1) + coef[6, here, :] * pltpu.roll(f, 1, 1)
        s = (s_old[here, :] + coef[7, here, :]) + (coef[0, here, :] * f + (x + (z + y)))
        s_new[here, :] = s
        if t < STEPS:
            f_new[plane(p, base), :] = tripled_fraction(s)

    sent = []

    def deliver(p, count):
        i = len(sent)
        here = plane(p, 0, count)
        onward = remote(s_even.at[here], received.at[here], end_send.at[i], end_recv.at[i], after)
        store = pltpu.make_async_copy(s_even.at[here], ends_hbm.at[here], out_sem.at[0, i])
        back = pltpu.make_async_copy(received.at[here], defects_hbm.at[here], out_sem.at[1, i])
        sent.append((p, count, onward, store, back))

        @pl.when(has_after)
        def _():
            onward.start()

        store.start()

    margin = half - 4 - STEPS

    @pl.loop(margin, last - margin + 1)
    def _(p):
        prepare(p)

    for t in range(1, STEPS + 1):

        @pl.loop(0, half - margin - t)
        def _(i):
            advance(margin + t + 2 * i, t)
            advance(margin + t + 2 * i + 1, t)

    deliver(half - 4, 8)

    @pl.loop(1, margin)
    def _(p):
        prepare(p)
        prepare(last - p)

    @pl.when(has_left)
    def _():
        first_right.wait_recv()
        face_right.wait_recv()

    @pl.when(has_right)
    def _():
        first_left.wait_recv()

    prepare(0)
    prepare(last)
    f_even[pl.ds(PAD, nz), :] = tripled_fraction(raw[0])
    f_even[pl.ds(base + rows, nz), :] = tripled_fraction(raw[1])

    halos = {}

    def exchange(t):
        f = f_odd if t % 2 else f_even
        to_left = remote(
            f.at[plane(0, base)], f.at[pl.ds(base + rows, nz)], halo_send.at[0, t], halo_recv.at[0, t], left
        )
        to_right = remote(
            f.at[plane(last, base)], f.at[pl.ds(PAD, nz)], halo_send.at[1, t], halo_recv.at[1, t], right
        )
        halos[t] = (to_left, to_right)

        @pl.when(has_left)
        def _():
            to_left.start()

        @pl.when(has_right)
        def _():
            to_right.start()

    def halo_arrived(t):
        @pl.when(has_left)
        def _():
            halos[t][1].wait_recv()

        @pl.when(has_right)
        def _():
            halos[t][0].wait_recv()

    def halo_left(t):
        @pl.when(has_left)
        def _():
            halos[t][0].wait_send()

        @pl.when(has_right)
        def _():
            halos[t][1].wait_send()

    advance(0, 1)
    advance(last, 1)
    exchange(1)

    for t in range(1, STEPS + 1):

        @pl.loop(0, margin)
        def _(i):
            advance(t + i, t)
            advance(last - t - i, t)

    deliver(STEPS, margin)
    deliver(nx - STEPS - margin, margin)

    for e in range(1, STEPS + 1):
        if e > 1:
            halo_arrived(e - 1)
            if e > 2:
                halo_left(e - 2)
            advance(0, e)
            advance(last, e)
            if e < STEPS:
                exchange(e)
        for j in range(1, STEPS + 1 - e):
            advance(j, e + j)
            advance(last - j, e + j)
        deliver(STEPS - e, 1)
        deliver(nx - 1 - STEPS + e, 1)
    halo_left(STEPS - 1)

    @pl.when(jnp.logical_not(has_before))
    def _():
        initial_load.wait()

    for p, count, onward, store, back in sent:
        here = plane(p, 0, count)

        @pl.when(has_before)
        def _():
            onward.wait_recv()

        received[here, :] = start[here, :] - received[here, :]
        back.start()

    @pl.when(has_left)
    def _():
        first_left.wait_send()

    @pl.when(has_right)
    def _():
        first_right.wait_send()
        face_right.wait_send()

    for p, count, onward, store, back in sent:

        @pl.when(has_after)
        def _():
            onward.wait_send()

        store.wait()
        back.wait()


def local(start, initial, ux, uy, uz, scale, cells, rates, roster):
    nx, nz, ny = ux.shape
    rows = nx * nz
    flat = (rows, ny)
    chunks = 3 + 2 * STEPS
    f32 = jnp.float32
    wide = (rows + 2 * nz + 2 * PAD, ny)
    dma = pltpu.SemaphoreType.DMA
    in_vmem = pl.BlockSpec(memory_space=pltpu.VMEM)
    anywhere = pl.BlockSpec(memory_space=pl.ANY)
    ends, defects = pl.pallas_call(
        functools.partial(kernel, nx, nz, ny),
        out_shape=[jax.ShapeDtypeStruct(flat, f32)] * 2,
        in_specs=[anywhere] * 6 + [in_vmem] * 3,
        out_specs=[anywhere] * 2,
        scratch_shapes=[
            pltpu.VMEM(flat, f32),
            pltpu.VMEM((rows + nz, ny), f32),
            pltpu.VMEM(flat, f32),
            pltpu.VMEM((rows + PAD, ny), f32),
            pltpu.VMEM(flat, f32),
            pltpu.VMEM(flat, f32),
            pltpu.VMEM(flat, f32),
            pltpu.VMEM(wide, f32),
            pltpu.VMEM(wide, f32),
            pltpu.VMEM((8,) + flat, f32),
            pltpu.VMEM(flat, f32),
            pltpu.VMEM(flat, f32),
            pltpu.VMEM(flat, f32),
            pltpu.VMEM((2, nz, ny), f32),
            dma((6,)),
            dma((2, chunks)),
            dma((3,)),
            dma((3,)),
            dma((2, STEPS)),
            dma((2, STEPS)),
            dma((chunks,)),
            dma((chunks,)),
        ],
        compiler_params=pltpu.CompilerParams(
            collective_id=0, has_side_effects=True, vmem_limit_bytes=40 << 20
        ),
    )(
        start.reshape(flat), initial.reshape(flat), ux.reshape(flat), uy.reshape(flat),
        uz.reshape(flat), scale.reshape(flat), cells, rates, roster.reshape(1, -1),
    )
    return ends.reshape(start.shape), defects.reshape(start.shape)


def solution(mesh):
    x_split = P("gx", None, None)
    both = P("shoot", "gx", None, None)
    return jax.shard_map(
        local,
        mesh=mesh,
        in_specs=(both,) + (x_split,) * 5 + (P("gx", None), P("gx", None), P("shoot", "gx", None)),
        out_specs=(both, both),
        check_vma=False,
    )
```

time: 197 us -> 51.5 us (0.26)
  other arithmetic: 75.1 us -> 0 us
  waiting for transfers between devices: 46 us -> 0 us
  starting transfers between devices: 41.3 us -> 0 us
  Pallas kernels: 0 us -> 40.5 us
  local copies, waits for them, and re-layouts: 31.8 us -> 9.95 us
    add x32 -> x0, other arithmetic: 56.4 us -> none  [the longest x16 30 us: face_flux(): jnp.maximum(velocity, 0.0) * here + jnp.minimum(velocity, 0.0) * there]
    ppermute x18 -> x0, waiting for transfers between devices: 46 us -> none  [the longest x2 24 us: passed_along(): return lax.ppermute(block, axis, route)]
    ppermute x18 -> x0, starting transfers between devices: 41.3 us -> none  [the longest x8 18.9 us: extended_2(): lax.ppermute(lax.slice_in_dim(block, block.shape[dim] - width, None, axis...]
    pallas_call x0 -> x1, Pallas kernels: none -> 40.5 us  [local(): pl.pallas_call(functools.partial(kernel, nx, nz, ny), out_shape=[jax.Shap...]
    slice x33 -> x0, local copies, waits for them, and re-layouts: 16.5 us -> none  [the longest x8 12.2 us: local(): x_face[:width - 1]]
    scatter-add x8 -> x0, other arithmetic: 13.4 us -> none  [well_sources(): return jnp.zeros_like(flow_flat).at[cells].add(terms)]
    gather x8 -> x0, local copies, waits for them, and re-layouts: 12 us -> none  [well_sources(): flow_flat[cells]]
    unnamed x46 -> x20, local copies, waits for them, and re-layouts: 3.28 us -> 9.95 us
  transfers between devices with their start and end apart: 18 -> 0, of which waited for: 9 -> 0; matrix products, arithmetic and copies ran while one was open for 3% -> 0% of each run, Pallas kernels for 0% -> 0%
where the time goes in v1:
time: 51.5 us; the launch traced here: 51.1 us
  Pallas kernels  40.5 us (79%)
  local copies, waits for them, and re-layouts  9.95 us (19%)
  between operations  0.67 us (1%)
    pallas_call x1, Pallas kernels, local(): pl.pallas_call(functools.partial(kernel, nx, nz, ny), out_shape=[jax.Shap...  40.5 us
    unnamed x20, local copies, waits for them, and re-layouts  9.95 us

profile of v1, /device:TPU:20, one launch (start us, length us, event | category | flops | bytes accessed | tf_op | source)
XLA Modules:
  0.0 51.1 jit_solution(15762872178176690869)
XLA Ops:
  0.6 0.0 copy-start.6
  0.6 0.0 copy-start.7
  0.7 0.0 copy-start.8
  0.7 0.6 %copy-done.6 = s32[1,16]{1,0:T(1,128)S(1)} copy-done((s32[1,16]{1,0:T(1,128)S(1)}, s32[1,16]{1,0:T(1,128)}, u32[]{:S(2)}) %copy-start.6) | copy-done | bytes 88
  1.3 0.0 copy-done.7
  1.3 0.0 copy-done.8
  1.3 0.0 copy-start
  1.3 1.2 %copy-done = f32[1,32,64,128]{3,2,1,0:T(8,128)S(1)} copy-done((f32[1,32,64,128]{3,2,1,0:T(8,128)S(1)}, f32[1,32,64,128]{3,2,1,0:T(8,128)}, u32[]{:S(2)}) %copy-start) | copy-done | bytes 1048600
  2.5 0.0 copy-start.1
  2.5 1.2 %copy-done.1 = f32[32,64,128]{2,1,0:T(8,128)S(1)} copy-done((f32[32,64,128]{2,1,0:T(8,128)S(1)}, f32[32,64,128]{2,1,0:T(8,128)}, u32[]{:S(2)}) %copy-start.1) | copy-done | bytes 1048600
  3.8 0.0 copy-start.2
  3.8 1.2 %copy-done.2 = f32[32,64,128]{2,1,0:T(8,128)S(1)} copy-done((f32[32,64,128]{2,1,0:T(8,128)S(1)}, f32[32,64,128]{2,1,0:T(8,128)}, u32[]{:S(2)}) %copy-start.2) | copy-done | bytes 1048600
  5.0 0.0 copy-start.3
  5.0 1.2 %copy-done.3 = f32[32,64,128]{2,1,0:T(8,128)S(1)} copy-done((f32[32,64,128]{2,1,0:T(8,128)S(1)}, f32[32,64,128]{2,1,0:T(8,128)}, u32[]{:S(2)}) %copy-start.3) | copy-done | bytes 1048600
  6.2 0.0 copy-start.4
  6.2 1.2 %copy-done.4 = f32[32,64,128]{2,1,0:T(8,128)S(1)} copy-done((f32[32,64,128]{2,1,0:T(8,128)S(1)}, f32[32,64,128]{2,1,0:T(8,128)}, u32[]{:S(2)}) %copy-start.4) | copy-done | bytes 1048600
  7.4 0.0 copy-start.5
  7.4 1.2 %copy-done.5 = f32[32,64,128]{2,1,0:T(8,128)S(1)} copy-done((f32[32,64,128]{2,1,0:T(8,128)S(1)}, f32[32,64,128]{2,1,0:T(8,128)}, u32[]{:S(2)}) %copy-start.5) | copy-done | bytes 1048600
  8.7 40.5 %shard_map.104 = (f32[2048,128]{1,0:T(8,128)S(1)}, f32[2048,128]{1,0:T(8,128)S(1)}) custom-call(f32[2048,128]{1,0:T(8,128)S(1)} %bitcast.11, f32[2048,128]{1,0:T(8,128)S(1)} %bitcast.12, f32[2048,128]{1,0:T(8,128)S(1)} %bitcast.13, f32[2048,128]{1,0:T(8,128)S(1)} %bitcast.14, f32[2048,128]{1,0:T(8,128)S(1)} %bitcast.15, f32[2048,128]{1,0:T(8,128)S(1)} %bitcast.16, ...), custom_call_target="tpu_custom_call" | custom-call | tf_op jit(solution)/shard_map/pallas_call | solution.py:322
  49.2 1.0 %copy.13 = f32[1,32,64,128]{3,2,1,0:T(8,128)} copy(f32[1,32,64,128]{3,2,1,0:T(8,128)S(1)} %bitcast.10) | data formatting | bytes 2097152
  50.2 1.0 %copy.14 = f32[1,32,64,128]{3,2,1,0:T(8,128)} copy(f32[1,32,64,128]{3,2,1,0:T(8,128)S(1)} %bitcast.9) | data formatting | bytes 2097152
Async XLA Ops:
  0.6 0.7 %copy-start.6 = (s32[1,16]{1,0:T(1,128)S(1)}, s32[1,16]{1,0:T(1,128)}, u32[]{:S(2)}) copy-start(s32[1,16]{1,0:T(1,128)} %cells_ref.1) | copy-start | bytes 196
  0.6 0.7 %copy-start.7 = (f32[1,16]{1,0:T(1,128)S(1)}, f32[1,16]{1,0:T(1,128)}, u32[]{:S(2)}) copy-start(f32[1,16]{1,0:T(1,128)} %rates_ref.1) | copy-start | bytes 196
  0.7 0.7 %copy-start.8 = (s32[1,1,16]{2,1,0:T(1,128)S(1)}, s32[1,1,16]{2,1,0:T(1,128)}, u32[]{:S(2)}) copy-start(s32[1,1,16]{2,1,0:T(1,128)} %param.17) | copy-start | bytes 196
  1.3 1.2 %copy-start = (f32[1,32,64,128]{3,2,1,0:T(8,128)S(1)}, f32[1,32,64,128]{3,2,1,0:T(8,128)}, u32[]{:S(2)}) copy-start(f32[1,32,64,128]{3,2,1,0:T(8,128)} %param.9) | copy-start | bytes 3145732
  2.5 1.2 %copy-start.1 = (f32[32,64,128]{2,1,0:T(8,128)S(1)}, f32[32,64,128]{2,1,0:T(8,128)}, u32[]{:S(2)}) copy-start(f32[32,64,128]{2,1,0:T(8,128)} %param.10) | copy-start | bytes 3145732
  3.8 1.2 %copy-start.2 = (f32[32,64,128]{2,1,0:T(8,128)S(1)}, f32[32,64,128]{2,1,0:T(8,128)}, u32[]{:S(2)}) copy-start(f32[32,64,128]{2,1,0:T(8,128)} %param.11) | copy-start | bytes 3145732
  5.0 1.2 %copy-start.3 = (f32[32,64,128]{2,1,0:T(8,128)S(1)}, f32[32,64,128]{2,1,0:T(8,128)}, u32[]{:S(2)}) copy-start(f32[32,64,128]{2,1,0:T(8,128)} %param.12) | copy-start | bytes 3145732
  6.2 1.2 %copy-start.4 = (f32[32,64,128]{2,1,0:T(8,128)S(1)}, f32[32,64,128]{2,1,0:T(8,128)}, u32[]{:S(2)}) copy-start(f32[32,64,128]{2,1,0:T(8,128)} %param.13) | copy-start | bytes 3145732
  7.4 1.2 %copy-start.5 = (f32[32,64,128]{2,1,0:T(8,128)S(1)}, f32[32,64,128]{2,1,0:T(8,128)}, u32[]{:S(2)}) copy-start(f32[32,64,128]{2,1,0:T(8,128)} %param.14) | copy-start | bytes 3145732
